TPU v7x, 32 devices: a whole 2x2x4 slice. The times are simulated.
32 devices in a mesh: rows: 32 (over z, y, x, core).
Axes of the slice: x: 2, y: 2, z: 4, core: 2. Of those that a mesh axis runs over, the one named last changes fastest.
Arguments:
- bases: float32 [5, 32768, 128], P(None, 'rows'), may hold values from -1 to 1
- targets: float32 [32768, 128], P('rows'), may hold values from -8 to 8
Outputs:
- solved: float32 [32768, 128], P('rows')
All inputs are finite; a program needn't handle non-finite values.
Results may differ from a plain program's by a relative error of at most 0.0001.
Values sent between devices are 32-bit elements; how exact they have to be, the bound alone decides.
A program may use at most 64 MiB of HBM per device.

v0:
```python
import functools

import jax
import jax.numpy as jnp
from jax import lax
from jax.experimental import pallas as pl
from jax.experimental.pallas import tpu as pltpu
from jax.sharding import PartitionSpec as P

AXIS = "rows"
VMEM_LIMIT = 48 * 2**20
VMEM_SPEC = pl.BlockSpec(memory_space=pltpu.VMEM)


def offset(level_no):
    return level_no * (level_no + 3) // 2


def split(value):
    high = value.astype(jnp.bfloat16)
    low = (value - high.astype(jnp.float32)).astype(jnp.bfloat16)
    return high, low


def dot_split(left, right):
    left_high, left_low = left
    right_high, right_low = right
    dot = functools.partial(jnp.dot, preferred_element_type=jnp.float32)
    return (dot(left_low, right_high) + dot(left_high, right_low)) + dot(left_high, right_high)


def dot3(left, right):
    return dot_split(split(left), split(right))


def wide(blocks):
    return jnp.concatenate(blocks, axis=1)


def gram_rows(bases_ref, targets_ref, store):
    levels = bases_ref.shape[0]
    rank = bases_ref.shape[2]
    parts = [split(targets_ref[...])]
    for level_no in range(levels):
        basis = bases_ref[level_no]
        parts.append(split(basis))
        turned = split(basis.T)
        rhs = (wide([part[0] for part in parts]), wide([part[1] for part in parts]))
        row = dot_split(turned, rhs)
        for col in range(level_no + 2):
            store(offset(level_no) + col, row[:, col * rank : (col + 1) * rank])


def eye(rank):
    shape = (rank, rank)
    row = lax.broadcasted_iota(jnp.int32, shape, 0)
    col = lax.broadcasted_iota(jnp.int32, shape, 1)
    return (row == col).astype(jnp.float32)


def square_step(inverse, power):
    rank = power.shape[0]
    both = dot3(power, wide([inverse, power]))
    return inverse + both[:, :rank], both[:, rank:]


def solve_pair(left_row, right_row, inverse_of):
    rank = left_row.shape[0]
    gram_a, gram_b = left_row[:, -rank:], right_row[:, -rank:]
    proj_a, proj_b = left_row[:, :-rank], right_row[:, :-rank]
    first = dot3(gram_a, wide([gram_b, proj_b]))
    inverse = inverse_of(first[:, :rank])
    coef_b = dot3(inverse, proj_a - first[:, rank:])
    coef_a = proj_b - dot3(gram_b, coef_b)
    return coef_a, coef_b


def adaptive_inverse(matrix):
    identity = eye(matrix.shape[0])

    def unfinished(state):
        step, _, power = state
        size = jnp.sum(power * power)
        return jnp.logical_and(size > 1e-14, step < 64)

    def body(state):
        step, inverse, power = state
        inverse, power = square_step(inverse, power)
        return step + 1, inverse, power

    state = (0, identity + matrix, dot3(matrix, matrix))
    return lax.while_loop(unfinished, body, state)[1]


def merged_rows(level_no, own, sib, sides, coef_a, coef_b, store):
    rank = coef_a.shape[0]
    proj_a, proj_b = sides[0][:, :-rank], sides[1][:, :-rank]
    stacked = jnp.concatenate([coef_a, coef_b], axis=0)
    rhs = split(jnp.concatenate([proj_a + coef_b, proj_b + coef_a], axis=0))
    for row_no in range(level_no):
        columns = slice((row_no + 1) * rank, (row_no + 2) * rank)
        turned = split(stacked[:, columns].T)
        end = (row_no + 2) * rank
        change = dot_split(turned, (rhs[0][:, :end], rhs[1][:, :end]))
        for col in range(row_no + 2):
            slot = offset(row_no) + col
            store(slot, own(slot) + sib(slot) - change[:, col * rank : (col + 1) * rank])


def final_coefs(coef_of, levels):
    deltas = []
    for level_no in range(levels):
        delta = coef_of(level_no, 0)
        if deltas:
            known = jnp.concatenate(deltas, axis=0)
            delta = delta - dot3(wide([coef_of(level_no, 1 + i) for i in range(level_no)]), known)
        deltas.append(delta)
    return deltas


def gram_kernel(bases_ref, targets_ref, out_ref):
    def store(slot, value):
        out_ref[slot] = value

    gram_rows(bases_ref, targets_ref, store)


def level_kernel(level_no, group_bits, own_ref, sib_ref, *out_refs):
    coef_ref = out_refs[0]
    is_left = lax.rem(lax.axis_index(AXIS) // 2**group_bits, 2) == 0
    base = offset(level_no)
    own_row = wide([own_ref[base + col] for col in range(level_no + 2)])
    sib_row = wide([sib_ref[base + col] for col in range(level_no + 2)])
    sides = (jnp.where(is_left, own_row, sib_row), jnp.where(is_left, sib_row, own_row))
    coef_a, coef_b = solve_pair(*sides, adaptive_inverse)
    own_coef = jnp.where(is_left, coef_a, coef_b)
    rank = coef_a.shape[0]
    for col in range(level_no + 1):
        coef_ref[col] = own_coef[:, col * rank : (col + 1) * rank]
    if level_no:
        next_ref = out_refs[1]

        def store(slot, value):
            next_ref[slot] = value

        merged_rows(
            level_no, lambda s: own_ref[s], lambda s: sib_ref[s], sides, coef_a, coef_b, store
        )


def apply_kernel(bases_ref, targets_ref, *refs):
    levels = bases_ref.shape[0]
    coefs, out_ref = refs[:-1], refs[-1]
    deltas = final_coefs(lambda level_no, col: coefs[level_no][col], levels)
    lhs = wide([bases_ref[level_no] for level_no in range(levels)])
    out_ref[...] = targets_ref[...] - dot3(lhs, jnp.concatenate(deltas, axis=0))


def call(kernel, outs, args):
    return pl.pallas_call(
        kernel,
        out_shape=outs,
        in_specs=[VMEM_SPEC] * len(args),
        out_specs=jax.tree.map(lambda _: VMEM_SPEC, outs),
        compiler_params=pltpu.CompilerParams(vmem_limit_bytes=VMEM_LIMIT),
    )(*args)


def from_partner(value, bit_no):
    pairs = [(source, source ^ 2**bit_no) for source in range(lax.axis_size(AXIS))]
    return lax.ppermute(value, AXIS, pairs)


def blocks(count, rank):
    return jax.ShapeDtypeStruct((count, rank, rank), jnp.float32)


def per_device(bases, targets):
    levels, _, rank = bases.shape
    tree_depth = lax.axis_size(AXIS).bit_length() - 1
    sums = call(gram_kernel, blocks(offset(levels), rank), (bases, targets))
    for bit_no in range(tree_depth - levels):
        sums = sums + from_partner(sums, bit_no)
    coefs = [None] * levels
    for level_no in reversed(range(levels)):
        group_bits = tree_depth - level_no - 1
        sibling = from_partner(sums, group_bits)
        outs = [blocks(level_no + 1, rank)]
        if level_no:
            outs.append(blocks(offset(level_no), rank))
        kernel = functools.partial(level_kernel, level_no, group_bits)
        coefs[level_no], *rest = call(kernel, tuple(outs), (sums, sibling))
        sums = rest[0] if rest else None
    out = jax.ShapeDtypeStruct(targets.shape, jnp.float32)
    return call(apply_kernel, out, (bases, targets, *coefs))


def solution(mesh):
    return jax.shard_map(
        per_device,
        mesh=mesh,
        in_specs=(P(None, AXIS, None), P(AXIS, None)),
        out_specs=P(AXIS, None),
        check_vma=False,
    )
```

profile of v0, /device:TPU:0, one launch (start us, length us, event | category | flops | bytes accessed | tf_op | source)
XLA Modules:
  0.0 76.3 jit_solution(4610597350507392328)
XLA Ops:
  0.0 0.0 copy-start
  0.0 1.7 %copy-done = f32[5,1024,128]{2,1,0:T(8,128)S(1)} copy-done((f32[5,1024,128]{2,1,0:T(8,128)S(1)}, f32[5,1024,128]{2,1,0:T(8,128)}, u32[]{:S(2)}) %copy-start) | copy-done | bytes 2621464
  1.7 0.0 copy-start.2
  1.7 1.0 %copy-done.2 = f32[1024,128]{1,0:T(8,128)S(1)} copy-done((f32[1024,128]{1,0:T(8,128)S(1)}, f32[1024,128]{1,0:T(8,128)}, u32[]{:S(2)}) %copy-start.2) | copy-done | bytes 524312
  2.8 2.5 %shard_map.28.own_ref = f32[20,128,128]{2,1,0:T(8,128)S(1)} custom-call(f32[5,1024,128]{2,1,0:T(8,128)S(1)} %copy-done, f32[1024,128]{1,0:T(8,128)S(1)} %copy-done.2), custom_call_target="tpu_custom_call" | custom-call | tf_op jit(solution)/shard_map/pallas_call | solution.py:160
  5.3 0.5 collective-permute-start
  5.8 2.7 %collective-permute-done.sib_ref = f32[20,128,128]{2,1,0:T(8,128)S(1)} collective-permute-done((f32[20,128,128]{2,1,0:T(8,128)S(1)}, f32[20,128,128]{2,1,0:T(8,128)S(1)}, u32[]{:S(2)}, u32[]{:S(2)}) %collective-permute-start) | collective-permute-done | bytes 1310752 | tf_op jit(solution)/shard_map/ppermute | solution.py:171
  8.5 2.5 %shard_map.29 = (f32[5,128,128]{2,1,0:T(8,128)S(1)}, f32[14,128,128]{2,1,0:T(8,128)S(1)}) custom-call(f32[20,128,128]{2,1,0:T(8,128)S(1)} %shard_map.28.own_ref, f32[20,128,128]{2,1,0:T(8,128)S(1)} %collective-permute-done.sib_ref), custom_call_target="tpu_custom_call" | custom-call | tf_op jit(solution)/shard_map/pallas_call | solution.py:160
  11.0 2.9 %collective-permute-start.1 = (f32[14,128,128]{2,1,0:T(8,128)S(1)}, f32[14,128,128]{2,1,0:T(8,128)S(1)}, u32[]{:S(2)}, u32[]{:S(2)}) collective-permute-start(f32[14,128,128]{2,1,0:T(8,128)S(1)} %get-tuple-element.13.own_ref), channel_id=1, source_target_pairs={{0,2},{1,3},{2,0},{3,1},{4,6},{5,7},{6,4},{7,5},{8,10},{9,11},{10,... | collective-permute-start | bytes 2752520 | tf_op jit(solution)/shard_map/ppermute | solution.py:171
  13.9 20.6 %collective-permute-done.1.sib_ref = f32[14,128,128]{2,1,0:T(8,128)S(1)} collective-permute-done((f32[14,128,128]{2,1,0:T(8,128)S(1)}, f32[14,128,128]{2,1,0:T(8,128)S(1)}, u32[]{:S(2)}, u32[]{:S(2)}) %collective-permute-start.1) | collective-permute-done | bytes 917536 | tf_op jit(solution)/shard_map/ppermute | solution.py:171
  34.6 0.0 copy-start.1
  34.6 2.2 %shard_map.30 = (f32[4,128,128]{2,1,0:T(8,128)S(1)}, f32[9,128,128]{2,1,0:T(8,128)S(1)}) custom-call(f32[14,128,128]{2,1,0:T(8,128)S(1)} %get-tuple-element.13.own_ref, f32[14,128,128]{2,1,0:T(8,128)S(1)} %collective-permute-done.1.sib_ref), custom_call_target="tpu_custom_call" | custom-call | tf_op jit(solution)/shard_map/pallas_call | solution.py:160
  36.8 0.0 copy-start.3
  36.8 1.8 %collective-permute-start.2 = (f32[9,128,128]{2,1,0:T(8,128)S(1)}, f32[9,128,128]{2,1,0:T(8,128)S(1)}, u32[]{:S(2)}, u32[]{:S(2)}) collective-permute-start(f32[9,128,128]{2,1,0:T(8,128)S(1)} %get-tuple-element.14.own_ref), channel_id=1, source_target_pairs={{0,4},{1,5},{2,6},{3,7},{4,0},{5,1},{6,2},{7,3},{8,12},{9,13},{10,... | collective-permute-start | bytes 1769480 | tf_op jit(solution)/shard_map/ppermute | solution.py:171
  38.6 13.1 %collective-permute-done.2.sib_ref = f32[9,128,128]{2,1,0:T(8,128)S(1)} collective-permute-done((f32[9,128,128]{2,1,0:T(8,128)S(1)}, f32[9,128,128]{2,1,0:T(8,128)S(1)}, u32[]{:S(2)}, u32[]{:S(2)}) %collective-permute-start.2) | collective-permute-done | bytes 589856 | tf_op jit(solution)/shard_map/ppermute | solution.py:171
  51.7 2.1 %shard_map.31 = (f32[3,128,128]{2,1,0:T(8,128)S(1)}, f32[5,128,128]{2,1,0:T(8,128)S(1)}) custom-call(f32[9,128,128]{2,1,0:T(8,128)S(1)} %get-tuple-element.14.own_ref, f32[9,128,128]{2,1,0:T(8,128)S(1)} %collective-permute-done.2.sib_ref), custom_call_target="tpu_custom_call" | custom-call | tf_op jit(solution)/shard_map/pallas_call | solution.py:160
  53.8 1.6 %collective-permute-start.3 = (f32[5,128,128]{2,1,0:T(8,128)S(1)}, f32[5,128,128]{2,1,0:T(8,128)S(1)}, u32[]{:S(2)}, u32[]{:S(2)}) collective-permute-start(f32[5,128,128]{2,1,0:T(8,128)S(1)} %get-tuple-element.15.own_ref), channel_id=1, source_target_pairs={{0,8},{1,9},{2,10},{3,11},{4,12},{5,13},{6,14},{7,15},{8,0},{9,1},... | collective-permute-start | bytes 983048 | tf_op jit(solution)/shard_map/ppermute | solution.py:171
  55.3 6.8 %collective-permute-done.3.sib_ref = f32[5,128,128]{2,1,0:T(8,128)S(1)} collective-permute-done((f32[5,128,128]{2,1,0:T(8,128)S(1)}, f32[5,128,128]{2,1,0:T(8,128)S(1)}, u32[]{:S(2)}, u32[]{:S(2)}) %collective-permute-start.3) | collective-permute-done | bytes 327712 | tf_op jit(solution)/shard_map/ppermute | solution.py:171
  62.2 2.2 %shard_map.32 = (f32[2,128,128]{2,1,0:T(8,128)S(1)}, f32[2,128,128]{2,1,0:T(8,128)S(1)}) custom-call(f32[5,128,128]{2,1,0:T(8,128)S(1)} %get-tuple-element.15.own_ref, f32[5,128,128]{2,1,0:T(8,128)S(1)} %collective-permute-done.3.sib_ref), custom_call_target="tpu_custom_call" | custom-call | tf_op jit(solution)/shard_map/pallas_call | solution.py:160
  64.4 2.3 %collective-permute-start.4 = (f32[2,128,128]{2,1,0:T(8,128)S(1)}, f32[2,128,128]{2,1,0:T(8,128)S(1)}, u32[]{:S(2)}, u32[]{:S(2)}) collective-permute-start(f32[2,128,128]{2,1,0:T(8,128)S(1)} %get-tuple-element.16.own_ref), channel_id=1, source_target_pairs={{0,16},{1,17},{2,18},{3,19},{4,20},{5,21},{6,22},{7,23},{8,24},{9,... | collective-permute-start | bytes 393224 | tf_op jit(solution)/shard_map/ppermute | solution.py:171
  66.6 5.1 %collective-permute-done.4.sib_ref = f32[2,128,128]{2,1,0:T(8,128)S(1)} collective-permute-done((f32[2,128,128]{2,1,0:T(8,128)S(1)}, f32[2,128,128]{2,1,0:T(8,128)S(1)}, u32[]{:S(2)}, u32[]{:S(2)}) %collective-permute-start.4) | collective-permute-done | bytes 131104 | tf_op jit(solution)/shard_map/ppermute | solution.py:171
  71.7 1.9 %shard_map.33.refs_0_ = f32[1,128,128]{2,1,0:T(8,128)S(1)} custom-call(f32[2,128,128]{2,1,0:T(8,128)S(1)} %get-tuple-element.16.own_ref, f32[2,128,128]{2,1,0:T(8,128)S(1)} %collective-permute-done.4.sib_ref), custom_call_target="tpu_custom_call" | custom-call | tf_op jit(solution)/shard_map/pallas_call | solution.py:160
  73.6 0.0 copy-done.1
  73.6 0.0 copy-done.3
  73.7 2.7 %shard_map.34 = f32[1024,128]{1,0:T(8,128)} custom-call(f32[5,1024,128]{2,1,0:T(8,128)S(1)} %copy-done.1, f32[1024,128]{1,0:T(8,128)S(1)} %copy-done.3, f32[1,128,128]{2,1,0:T(8,128)S(1)} %shard_map.33.refs_0_, f32[2,128,128]{2,1,0:T(8,128)S(1)} %get-tuple-element.17.refs_1_, f32[3,128,128]{2,1,0:T(8,128)S(1)} %get-tuple-element.18.refs_2_, ...), custom_call_target="tpu_custom_call" | custom-call | tf_op jit(solution)/shard_map/pallas_call | solution.py:160
Async XLA Ops:
  0.0 1.7 %copy-start = (f32[5,1024,128]{2,1,0:T(8,128)S(1)}, f32[5,1024,128]{2,1,0:T(8,128)}, u32[]{:S(2)}) copy-start(f32[5,1024,128]{2,1,0:T(8,128)} %bases_ref.3) | copy-start | bytes 7864324
  1.7 1.0 %copy-start.2 = (f32[1024,128]{1,0:T(8,128)S(1)}, f32[1024,128]{1,0:T(8,128)}, u32[]{:S(2)}) copy-start(f32[1024,128]{1,0:T(8,128)} %targets_ref.3) | copy-start | bytes 1572868
  5.3 3.2 %collective-permute-start = (f32[20,128,128]{2,1,0:T(8,128)S(1)}, f32[20,128,128]{2,1,0:T(8,128)S(1)}, u32[]{:S(2)}, u32[]{:S(2)}) collective-permute-start(f32[20,128,128]{2,1,0:T(8,128)S(1)} %shard_map.28.own_ref), channel_id=1, source_target_pairs={{0,1},{1,0},{2,3},{3,2},{4,5},{5,4},{6,7},{7,6},{8,9},{9,8},{10,11... | collective-permute-start | bytes 3932168 | tf_op jit(solution)/shard_map/ppermute | solution.py:171
  11.0 23.6 %collective-permute-start.1 = (f32[14,128,128]{2,1,0:T(8,128)S(1)}, f32[14,128,128]{2,1,0:T(8,128)S(1)}, u32[]{:S(2)}, u32[]{:S(2)}) collective-permute-start(f32[14,128,128]{2,1,0:T(8,128)S(1)} %get-tuple-element.13.own_ref), channel_id=1, source_target_pairs={{0,2},{1,3},{2,0},{3,1},{4,6},{5,7},{6,4},{7,5},{8,10},{9,11},{10,... | collective-permute-start | bytes 2752520 | tf_op jit(solution)/shard_map/ppermute | solution.py:171
  34.6 39.1 %copy-start.1 = (f32[5,1024,128]{2,1,0:T(8,128)S(1)}, f32[5,1024,128]{2,1,0:T(8,128)}, u32[]{:S(2)}) copy-start(f32[5,1024,128]{2,1,0:T(8,128)} %bases_ref.3) | copy-start | bytes 7864324
  36.8 36.9 %copy-start.3 = (f32[1024,128]{1,0:T(8,128)S(1)}, f32[1024,128]{1,0:T(8,128)}, u32[]{:S(2)}) copy-start(f32[1024,128]{1,0:T(8,128)} %targets_ref.3) | copy-start | bytes 1572868
  36.8 14.9 %collective-permute-start.2 = (f32[9,128,128]{2,1,0:T(8,128)S(1)}, f32[9,128,128]{2,1,0:T(8,128)S(1)}, u32[]{:S(2)}, u32[]{:S(2)}) collective-permute-start(f32[9,128,128]{2,1,0:T(8,128)S(1)} %get-tuple-element.14.own_ref), channel_id=1, source_target_pairs={{0,4},{1,5},{2,6},{3,7},{4,0},{5,1},{6,2},{7,3},{8,12},{9,13},{10,... | collective-permute-start | bytes 1769480 | tf_op jit(solution)/shard_map/ppermute | solution.py:171
  53.8 8.4 %collective-permute-start.3 = (f32[5,128,128]{2,1,0:T(8,128)S(1)}, f32[5,128,128]{2,1,0:T(8,128)S(1)}, u32[]{:S(2)}, u32[]{:S(2)}) collective-permute-start(f32[5,128,128]{2,1,0:T(8,128)S(1)} %get-tuple-element.15.own_ref), channel_id=1, source_target_pairs={{0,8},{1,9},{2,10},{3,11},{4,12},{5,13},{6,14},{7,15},{8,0},{9,1},... | collective-permute-start | bytes 983048 | tf_op jit(solution)/shard_map/ppermute | solution.py:171
  64.4 7.3 %collective-permute-start.4 = (f32[2,128,128]{2,1,0:T(8,128)S(1)}, f32[2,128,128]{2,1,0:T(8,128)S(1)}, u32[]{:S(2)}, u32[]{:S(2)}) collective-permute-start(f32[2,128,128]{2,1,0:T(8,128)S(1)} %get-tuple-element.16.own_ref), channel_id=1, source_target_pairs={{0,16},{1,17},{2,18},{3,19},{4,20},{5,21},{6,22},{7,23},{8,24},{9,... | collective-permute-start | bytes 393224 | tf_op jit(solution)/shard_map/ppermute | solution.py:171
where the time goes:
time: 76.5 us; the launch traced here: 76.3 us
  waiting for transfers between devices  48.3 us (63%)
  Pallas kernels  16 us (21%)
  starting transfers between devices  9.1 us (12%)
  local copies, waits for them, and re-layouts  2.79 us (4%)
    ppermute x5, waiting for transfers between devices, from_partner(): return lax.ppermute(value, AXIS, pairs)  48.3 us
    pallas_call x7, Pallas kernels, call(): pl.pallas_call(kernel, out_shape=outs, in_specs=[VMEM_SPEC] * len(args),...  16 us
    ppermute x5, starting transfers between devices, from_partner(): return lax.ppermute(value, AXIS, pairs)  9.1 us
    unnamed x8, local copies, waits for them, and re-layouts  2.79 us
  transfers between devices with their start and end apart: 5, of which 5 were waited for; matrix products, arithmetic and copies ran while one was open for 0% of the time, Pallas kernels for 0%

commit v1 on v0

--- a/solution.py
+++ b/solution.py
@@ -175,7 +175,192 @@
     return jax.ShapeDtypeStruct((count, rank, rank), jnp.float32)
 
 
-def per_device(bases, targets):
+SQUARINGS = 4
+RESIDUAL = 1e-9
+
+
+def fixed_inverse(matrix):
+    inverse, power = eye(matrix.shape[0]) + matrix, dot3(matrix, matrix)
+    for _ in range(SQUARINGS):
+        inverse, power = square_step(inverse, power)
+    return inverse, power
+
+
+def fused_kernel(depth, bases_ref, targets_ref, out_ref, flag_ref, *refs):
+    levels, _, rank = bases_ref.shape
+    half = rank // 2
+    sums, taken = refs[:depth], refs[depth : 2 * depth]
+    coef, turned_ref, moved, flag_own, flag_in = refs[2 * depth : 2 * depth + 5]
+    sems = refs[2 * depth + 5 :]
+    link_send, link_recv, core_send, core_recv, relay_send, relay_recv, flag_send, flag_recv = sems
+    me = lax.axis_index(AXIS)
+    core = lax.rem(me, 2)
+    own_half = pl.ds(pl.multiple_of(core * half, half), half)
+    other_half = pl.ds(pl.multiple_of((1 - core) * half, half), half)
+    pending = []
+
+    def side(bit):
+        return lax.rem(me // 2**bit, 2)
+
+    def partner(bit):
+        return me + 2**bit * (1 - 2 * side(bit))
+
+    def push(src, dst, send, recv, bit):
+        copy = pltpu.make_async_remote_copy(
+            src_ref=src,
+            dst_ref=dst,
+            send_sem=send,
+            recv_sem=recv,
+            device_id=(partner(bit),),
+            device_id_type=pl.DeviceIdType.MESH,
+        )
+        copy.start()
+        pending.append(copy)
+        return copy
+
+    barrier = pltpu.get_barrier_semaphore()
+    for bit in range(depth):
+        pl.semaphore_signal(
+            barrier, inc=1, device_id=(partner(bit),), device_id_type=pl.DeviceIdType.MESH
+        )
+
+    links, swaps = {}, {}
+
+    def send_row(bit, row):
+        slots = pl.ds(offset(row), row + 2)
+        critical = row == depth - 1 - bit
+        if bit == 0:
+            region = (slots,) if critical else (slots, other_half)
+        else:
+            region = (slots, own_half)
+        src, dst = sums[bit].at[region], taken[bit].at[region]
+        links[bit, row] = push(src, dst, link_send.at[bit, row], link_recv.at[bit, row], bit)
+        if critical and bit:
+            swaps[bit] = push(src, src, core_send.at[bit], core_recv.at[bit], 0)
+
+    parts = [split(targets_ref[...])] + [split(bases_ref[i]) for i in range(levels)]
+    high, low = wide([part[0] for part in parts]), wide([part[1] for part in parts])
+    for row in reversed(range(levels)):
+        end = (row + 2) * rank
+        value = dot_split(split(bases_ref[row].T), (high[:, :end], low[:, :end]))
+        for col in range(row + 2):
+            sums[0][offset(row) + col] = value[:, col * rank : (col + 1) * rank]
+        if row == levels - 1:
+            pl.semaphore_wait(barrier, depth)
+        send_row(0, row)
+
+    def coef_slot(level_no, col):
+        return level_no * (level_no + 1) // 2 + col
+
+    def move_rows():
+        deltas = []
+        for level_no in range(1, levels):
+            delta = wide([coef[coef_slot(level_no, col)] for col in range(2)])
+            if deltas:
+                lhs = wide([coef[coef_slot(level_no, 1 + i)] for i in range(1, level_no)])
+                delta = delta - dot3(lhs, jnp.concatenate(deltas, axis=0))
+            deltas.append(delta)
+        change = dot_split((high[:, 2 * rank :], low[:, 2 * rank :]), split(jnp.concatenate(deltas, axis=0)))
+        moved[:, :rank] = targets_ref[...] - change[:, :rank]
+        moved[:, rank:] = bases_ref[0] - change[:, rank:]
+
+    flag = jnp.zeros((8, 128), jnp.float32)
+    for bit in range(depth):
+        level_no = depth - 1 - bit
+        solving = level_no < levels
+        if bit:
+            flag_own[bit] = flag
+            flag_copy = push(
+                flag_own.at[bit], flag_in.at[bit], flag_send.at[bit], flag_recv.at[bit], bit
+            )
+        if level_no == 0:
+            move_rows()
+        if solving:
+            slots = pl.ds(offset(level_no), level_no + 2)
+            links[bit, level_no].wait_recv()
+            if bit:
+                region = taken[bit].at[slots, own_half]
+                relay = push(region, region, relay_send.at[bit], relay_recv.at[bit], 0)
+                swaps[bit].wait_recv()
+                relay.wait_recv()
+            base = offset(level_no)
+            own_row = wide([sums[bit][base + col] for col in range(level_no + 2)])
+            sib_row = wide([taken[bit][base + col] for col in range(level_no + 2)])
+            is_left = side(bit) == 0
+            left_row = jnp.where(is_left, own_row, sib_row)
+            right_row = jnp.where(is_left, sib_row, own_row)
+            state = []
+
+            def inverse_of(matrix):
+                inverse, power = fixed_inverse(matrix)
+                state.append(jnp.max((power * power).reshape(rank // 8, 8, rank), axis=0))
+                return inverse
+
+            coef_a, coef_b = solve_pair(left_row, right_row, inverse_of)
+            flag = jnp.maximum(flag, state[0])
+            own_coef = jnp.where(is_left, coef_a, coef_b)
+            if level_no == 0:
+                out_ref[...] = moved[:, :rank] - dot3(moved[:, rank:], own_coef)
+            for col in range(level_no + 1):
+                coef[coef_slot(level_no, col)] = own_coef[:, col * rank : (col + 1) * rank]
+            if level_no:
+                proj_a, proj_b = left_row[:, :-rank], right_row[:, :-rank]
+                stacked = jnp.concatenate([coef_a, coef_b], axis=0)
+                rhs = split(jnp.concatenate([proj_a + coef_b, proj_b + coef_a], axis=0))
+        for row in reversed(range(min(level_no, levels))):
+            if solving:
+                turned_ref[...] = stacked[:, (row + 1) * rank : (row + 2) * rank].T
+                end = (row + 2) * rank
+                change = dot_split(split(turned_ref[own_half, :]), (rhs[0][:, :end], rhs[1][:, :end]))
+            links[bit, row].wait_recv()
+            for col in range(row + 2):
+                slot = offset(row) + col
+                value = sums[bit][slot, own_half, :] + taken[bit][slot, own_half, :]
+                if solving:
+                    value = value - change[:, col * rank : (col + 1) * rank]
+                sums[bit + 1][slot, own_half, :] = value
+            send_row(bit + 1, row)
+        if bit:
+            flag_copy.wait_recv()
+            flag = jnp.maximum(flag, flag_in[bit])
+    flag_ref[...] = flag
+    for copy in pending:
+        copy.wait_send()
+
+
+def fused(bases, targets, depth):
+    levels, rows, rank = bases.shape
+    stages = [
+        pltpu.VMEM((offset(min(depth - bit, levels)), rank, rank), jnp.float32)
+        for bit in range(depth)
+    ]
+    dma = pltpu.SemaphoreType.DMA
+    return pl.pallas_call(
+        functools.partial(fused_kernel, depth),
+        out_shape=(
+            jax.ShapeDtypeStruct(targets.shape, jnp.float32),
+            jax.ShapeDtypeStruct((8, 128), jnp.float32),
+        ),
+        in_specs=[VMEM_SPEC] * 2,
+        out_specs=(VMEM_SPEC, VMEM_SPEC),
+        scratch_shapes=stages
+        + stages
+        + [
+            pltpu.VMEM((levels * (levels + 1) // 2, rank, rank), jnp.float32),
+            pltpu.VMEM((rank, 2 * rank), jnp.float32),
+            pltpu.VMEM((rows, 2 * rank), jnp.float32),
+            pltpu.VMEM((depth, 8, 128), jnp.float32),
+            pltpu.VMEM((depth, 8, 128), jnp.float32),
+        ]
+        + [dma((depth, levels))] * 2
+        + [dma((depth,))] * 6,
+        compiler_params=pltpu.CompilerParams(
+            collective_id=0, has_side_effects=True, vmem_limit_bytes=VMEM_LIMIT
+        ),
+    )(bases, targets)
+
+
+def general(bases, targets):
     levels, _, rank = bases.shape
     tree_depth = lax.axis_size(AXIS).bit_length() - 1
     sums = call(gram_kernel, blocks(offset(levels), rank), (bases, targets))
@@ -195,6 +380,15 @@
     return call(apply_kernel, out, (bases, targets, *coefs))
 
 
+def per_device(bases, targets):
+    depth = lax.axis_size(AXIS).bit_length() - 1
+    out, residual = fused(bases, targets, depth)
+    limit = (RESIDUAL / bases.shape[2]) ** 2
+    return lax.cond(
+        jnp.max(residual) < limit, lambda b, t, o: o, lambda b, t, o: general(b, t), bases, targets, out
+    )
+
+
 def solution(mesh):
     return jax.shard_map(
         per_device,

time: 76.5 us -> 51.4 us (0.67)
  waiting for transfers between devices: 48.3 us -> 0 us
  Pallas kernels: 16 us -> 47.9 us
  starting transfers between devices: 9.1 us -> 0 us
  local copies, waits for them, and re-layouts: 2.79 us -> 1.88 us
    ppermute x5 -> x0, waiting for transfers between devices: 48.3 us -> none  [from_partner(): return lax.ppermute(value, AXIS, pairs)]
    pallas_call x7 -> x1, Pallas kernels: 16 us -> 47.9 us  [fused(): pl.pallas_call(functools.partial(fused_kernel, depth), out_shape=(jax.Sha...]
    ppermute x5 -> x0, starting transfers between devices: 9.1 us -> none  [from_partner(): return lax.ppermute(value, AXIS, pairs)]
    unnamed x8 -> x5, local copies, waits for them, and re-layouts: 2.79 us -> 1.88 us
  transfers between devices with their start and end apart: 5 -> 0, of which waited for: 5 -> 0; matrix products, arithmetic and copies ran while one was open for 0% -> 0% of each run, Pallas kernels for 0% -> 0%
where the time goes in v1:
time: 51.4 us; the launch traced here: 51.2 us
  Pallas kernels  47.9 us (93%)
  local copies, waits for them, and re-layouts  1.88 us (4%)
  between operations  0.69 us (1%)
  other arithmetic  0.6 us (1%)
    pallas_call x1, Pallas kernels, fused(): pl.pallas_call(functools.partial(fused_kernel, depth), out_shape=(jax.Sha...  47.9 us
    unnamed x5, local copies, waits for them, and re-layouts  1.88 us

profile of v1, /device:TPU:0, one launch (start us, length us, event | category | flops | bytes accessed | tf_op | source)
XLA Modules:
  0.0 51.2 jit_solution(3783420351265337087)
XLA Ops:
  0.0 0.0 copy-start
  0.0 0.0 copy-start.1
  0.0 47.9 %shard_map.30 = (f32[1024,128]{1,0:T(8,128)}, f32[8,128]{1,0:T(8,128)S(1)}) custom-call(f32[5,1024,128]{2,1,0:T(8,128)} %bases_ref.1, f32[1024,128]{1,0:T(8,128)} %targets_ref.1), custom_call_target="tpu_custom_call" | custom-call | tf_op jit(solution)/shard_map/pallas_call | solution.py:338
  47.9 0.6 %reduce_max.9 = f32[]{:T(128)} reduce(f32[8,128]{1,0:T(8,128)S(1)} %get-tuple-element.25, f32[]{:T(128)} %constant.0.clone.1), dimensions={0,1}, to_apply=%region_0.0 | reduce | flops 1023 | bytes 4104 | tf_op jit(solution)/shard_map/reduce_max | solution.py:388
  49.1 0.0 copy-done
  49.1 0.0 copy-done.1
  49.1 0.2 conditional.1
  49.4 1.9 %copy.8 = f32[1024,128]{1,0:T(8,128)} copy(f32[1024,128]{1,0:T(8,128)} %get-tuple-element.27) | data formatting | bytes 1048576
Async XLA Ops:
  0.0 49.1 %copy-start = (f32[5,1024,128]{2,1,0:T(8,128)S(1)}, f32[5,1024,128]{2,1,0:T(8,128)}, u32[]{:S(2)}) copy-start(f32[5,1024,128]{2,1,0:T(8,128)} %bases_ref.1) | copy-start | bytes 7864324
  0.0 49.1 %copy-start.1 = (f32[1024,128]{1,0:T(8,128)S(1)}, f32[1024,128]{1,0:T(8,128)}, u32[]{:S(2)}) copy-start(f32[1024,128]{1,0:T(8,128)} %targets_ref.1) | copy-start | bytes 1572868

commit v2 on v1

--- a/solution.py
+++ b/solution.py
@@ -186,12 +186,12 @@
     return inverse, power
 
 
-def fused_kernel(depth, bases_ref, targets_ref, out_ref, flag_ref, *refs):
+def fused_kernel(depth, bases_ref, targets_ref, moved, last_ref, flag_ref, *refs):
     levels, _, rank = bases_ref.shape
     half = rank // 2
     sums, taken = refs[:depth], refs[depth : 2 * depth]
-    coef, turned_ref, moved, flag_own, flag_in = refs[2 * depth : 2 * depth + 5]
-    sems = refs[2 * depth + 5 :]
+    coef, turned_ref, flag_own, flag_in = refs[2 * depth : 2 * depth + 4]
+    sems = refs[2 * depth + 4 :]
     link_send, link_recv, core_send, core_recv, relay_send, relay_recv, flag_send, flag_recv = sems
     me = lax.axis_index(AXIS)
     core = lax.rem(me, 2)
@@ -264,10 +264,34 @@
         moved[:, :rank] = targets_ref[...] - change[:, :rank]
         moved[:, rank:] = bases_ref[0] - change[:, rank:]
 
+    def merge_row(bit, row, change_of):
+        links[bit, row].wait_recv()
+        change = change_of(row)
+        for col in range(row + 2):
+            slot = offset(row) + col
+            value = sums[bit][slot, own_half, :] + taken[bit][slot, own_half, :]
+            if change is not None:
+                value = value - change[:, col * rank : (col + 1) * rank]
+            sums[bit + 1][slot, own_half, :] = value
+
+    def changes(coef_a, coef_b, left_row, right_row):
+        proj_a, proj_b = left_row[:, :-rank], right_row[:, :-rank]
+        stacked = jnp.concatenate([coef_a, coef_b], axis=0)
+        rhs = split(jnp.concatenate([proj_a + coef_b, proj_b + coef_a], axis=0))
+
+        def change_of(row):
+            turned_ref[...] = stacked[:, (row + 1) * rank : (row + 2) * rank].T
+            end = (row + 2) * rank
+            return dot_split(split(turned_ref[own_half, :]), (rhs[0][:, :end], rhs[1][:, :end]))
+
+        return change_of
+
     flag = jnp.zeros((8, 128), jnp.float32)
+    late, late_change = [], None
     for bit in range(depth):
         level_no = depth - 1 - bit
         solving = level_no < levels
+        rest = list(reversed(range(min(level_no, levels))))
         if bit:
             flag_own[bit] = flag
             flag_copy = push(
@@ -275,12 +299,18 @@
             )
         if level_no == 0:
             move_rows()
+        change_of = lambda row: None
         if solving:
             slots = pl.ds(offset(level_no), level_no + 2)
             links[bit, level_no].wait_recv()
             if bit:
                 region = taken[bit].at[slots, own_half]
                 relay = push(region, region, relay_send.at[bit], relay_recv.at[bit], 0)
+            for row in late:
+                merge_row(bit - 1, row, late_change)
+                if row == rest[0]:
+                    send_row(bit, row)
+            if bit:
                 swaps[bit].wait_recv()
                 relay.wait_recv()
             base = offset(level_no)
@@ -299,33 +329,33 @@
             coef_a, coef_b = solve_pair(left_row, right_row, inverse_of)
             flag = jnp.maximum(flag, state[0])
             own_coef = jnp.where(is_left, coef_a, coef_b)
-            if level_no == 0:
-                out_ref[...] = moved[:, :rank] - dot3(moved[:, rank:], own_coef)
             for col in range(level_no + 1):
                 coef[coef_slot(level_no, col)] = own_coef[:, col * rank : (col + 1) * rank]
-            if level_no:
-                proj_a, proj_b = left_row[:, :-rank], right_row[:, :-rank]
-                stacked = jnp.concatenate([coef_a, coef_b], axis=0)
-                rhs = split(jnp.concatenate([proj_a + coef_b, proj_b + coef_a], axis=0))
-        for row in reversed(range(min(level_no, levels))):
-            if solving:
-                turned_ref[...] = stacked[:, (row + 1) * rank : (row + 2) * rank].T
-                end = (row + 2) * rank
-                change = dot_split(split(turned_ref[own_half, :]), (rhs[0][:, :end], rhs[1][:, :end]))
-            links[bit, row].wait_recv()
-            for col in range(row + 2):
-                slot = offset(row) + col
-                value = sums[bit][slot, own_half, :] + taken[bit][slot, own_half, :]
-                if solving:
-                    value = value - change[:, col * rank : (col + 1) * rank]
-                sums[bit + 1][slot, own_half, :] = value
-            send_row(bit + 1, row)
+            if level_no == 0:
+                last_ref[...] = own_coef
+            else:
+                change_of = changes(coef_a, coef_b, left_row, right_row)
+        if rest:
+            following = level_no - 1 < levels
+            for row in rest[:1] if following else rest:
+                merge_row(bit, row, change_of)
+                send_row(bit + 1, row)
+            late = rest[1:] if following else []
+            late_change = change_of
+            for row in late:
+                if (bit, row) not in links:
+                    send_row(bit, row)
         if bit:
             flag_copy.wait_recv()
             flag = jnp.maximum(flag, flag_in[bit])
     flag_ref[...] = flag
     for copy in pending:
         copy.wait_send()
+
+
+def finish_kernel(moved_ref, last_ref, out_ref):
+    rank = last_ref.shape[0]
+    out_ref[...] = moved_ref[:, :rank] - dot3(moved_ref[:, rank:], last_ref[...])
 
 
 def fused(bases, targets, depth):
@@ -338,17 +368,17 @@
     return pl.pallas_call(
         functools.partial(fused_kernel, depth),
         out_shape=(
-            jax.ShapeDtypeStruct(targets.shape, jnp.float32),
+            jax.ShapeDtypeStruct((rows, 2 * rank), jnp.float32),
+            jax.ShapeDtypeStruct((rank, rank), jnp.float32),
             jax.ShapeDtypeStruct((8, 128), jnp.float32),
         ),
         in_specs=[VMEM_SPEC] * 2,
-        out_specs=(VMEM_SPEC, VMEM_SPEC),
+        out_specs=(VMEM_SPEC,) * 3,
         scratch_shapes=stages
         + stages
         + [
             pltpu.VMEM((levels * (levels + 1) // 2, rank, rank), jnp.float32),
             pltpu.VMEM((rank, 2 * rank), jnp.float32),
-            pltpu.VMEM((rows, 2 * rank), jnp.float32),
             pltpu.VMEM((depth, 8, 128), jnp.float32),
             pltpu.VMEM((depth, 8, 128), jnp.float32),
         ]
@@ -382,10 +412,13 @@
 
 def per_device(bases, targets):
     depth = lax.axis_size(AXIS).bit_length() - 1
-    out, residual = fused(bases, targets, depth)
+    moved, last, residual = fused(bases, targets, depth)
     limit = (RESIDUAL / bases.shape[2]) ** 2
+    out = jax.ShapeDtypeStruct(targets.shape, jnp.float32)
     return lax.cond(
-        jnp.max(residual) < limit, lambda b, t, o: o, lambda b, t, o: general(b, t), bases, targets, out
+        jnp.max(residual) < limit,
+        lambda: call(finish_kernel, out, (moved, last)),
+        lambda: general(bases, targets),
     )
 
 

time: 51.4 us -> 51.7 us (level)
  local copies, waits for them, and re-layouts: 1.88 us -> 0.8 us
  Pallas kernels: 47.9 us -> 48.9 us
    pallas_call x0 -> x1, Pallas kernels: none -> 1.58 us  [call(): pl.pallas_call(kernel, out_shape=outs, in_specs=[VMEM_SPEC] * len(args),...]
    unnamed x5 -> x6, local copies, waits for them, and re-layouts: 1.88 us -> 0.8 us
where the time goes in v2:
time: 51.7 us; the launch traced here: 51.3 us
  Pallas kernels  48.9 us (95%)
  local copies, waits for them, and re-layouts  0.8 us (2%)
  between operations  0.7 us (1%)
  other arithmetic  0.6 us (1%)
    pallas_call x1, Pallas kernels, fused(): pl.pallas_call(functools.partial(fused_kernel, depth), out_shape=(jax.Sha...  47.4 us
    pallas_call x1, Pallas kernels, call(): pl.pallas_call(kernel, out_shape=outs, in_specs=[VMEM_SPEC] * len(args),...  1.58 us

profile of v2, /device:TPU:0, one launch (start us, length us, event | category | flops | bytes accessed | tf_op | source)
XLA Modules:
  0.0 51.3 jit_solution(17353871980787492935)
XLA Ops:
  0.0 0.0 copy-start
  0.0 0.0 copy-start.1
  0.0 47.4 %shard_map.30 = (f32[1024,256]{1,0:T(8,128)}, f32[128,128]{1,0:T(8,128)S(1)}, f32[8,128]{1,0:T(8,128)S(1)}) custom-call(f32[5,1024,128]{2,1,0:T(8,128)} %bases_ref.1, f32[1024,128]{1,0:T(8,128)} %targets_ref.1), custom_call_target="tpu_custom_call" | custom-call | tf_op jit(solution)/shard_map/pallas_call | solution.py:368
  47.4 0.6 %reduce_max.9 = f32[]{:T(128)} reduce(f32[8,128]{1,0:T(8,128)S(1)} %get-tuple-element.31, f32[]{:T(128)} %constant.0.clone.1), dimensions={0,1}, to_apply=%region_0.0 | reduce | flops 1023 | bytes 4104 | tf_op jit(solution)/shard_map/reduce_max | solution.py:419
  48.6 0.0 copy-done
  48.6 0.0 copy-done.1
  48.6 1.8 %conditional.1 = (f32[1024,128]{1,0:T(8,128)S(1)}) conditional(s32[]{:T(128)} %convert_element_type.3, (f32[5,1024,128]{2,1,0:T(8,128)S(1)}, f32[1024,128]{1,0:T(8,128)S(1)}) %tuple.18, (f32[1024,256]{1,0:T(8,128)}, f32[128,128]{1,0:T(8,128)S(1)}) %tuple.12), branch_computations={%region_1.0_spmd, %region_2.0_spmd} | conditional | bytes 13107408 | solution.py:418
  48.9 1.6 %branch_1_fun.1 = f32[1024,128]{1,0:T(8,128)S(1)} custom-call(f32[1024,256]{1,0:T(8,128)} %get-tuple-element.26.moved_ref, f32[128,128]{1,0:T(8,128)S(1)} %get-tuple-element.27.last_ref), custom_call_target="tpu_custom_call" | custom-call | tf_op jit(solution)/shard_map/cond/branch_1_fun/pallas_call | solution.py:160
  50.5 0.0 copy-start.2
  50.5 0.8 %copy-done.2 = f32[1024,128]{1,0:T(8,128)} copy-done((f32[1024,128]{1,0:T(8,128)}, f32[1024,128]{1,0:T(8,128)S(1)}, u32[]{:S(2)}) %copy-start.2) | copy-done | bytes 524312
Async XLA Ops:
  0.0 48.6 %copy-start = (f32[5,1024,128]{2,1,0:T(8,128)S(1)}, f32[5,1024,128]{2,1,0:T(8,128)}, u32[]{:S(2)}) copy-start(f32[5,1024,128]{2,1,0:T(8,128)} %bases_ref.1) | copy-start | bytes 7864324
  0.0 48.6 %copy-start.1 = (f32[1024,128]{1,0:T(8,128)S(1)}, f32[1024,128]{1,0:T(8,128)}, u32[]{:S(2)}) copy-start(f32[1024,128]{1,0:T(8,128)} %targets_ref.1) | copy-start | bytes 1572868
  50.5 0.8 %copy-start.2 = (f32[1024,128]{1,0:T(8,128)}, f32[1024,128]{1,0:T(8,128)S(1)}, u32[]{:S(2)}) copy-start(f32[1024,128]{1,0:T(8,128)S(1)} %get-tuple-element.47) | copy-start | bytes 1572868

commit v3 on v2

--- a/solution.py
+++ b/solution.py
@@ -175,8 +175,8 @@
     return jax.ShapeDtypeStruct((count, rank, rank), jnp.float32)
 
 
-SQUARINGS = 4
-RESIDUAL = 1e-9
+SQUARINGS = 3
+RESIDUAL = 1e-7
 
 
 def fixed_inverse(matrix):
@@ -186,12 +186,22 @@
     return inverse, power
 
 
-def fused_kernel(depth, bases_ref, targets_ref, moved, last_ref, flag_ref, *refs):
+def inverse_of_pair(gram_a, gram_b):
+    rank = gram_a.shape[0]
+    parts_a, parts_b = split(gram_a), split(gram_b)
+    inverse, power = fixed_inverse(dot_split(parts_a, parts_b))
+    weighted = dot_split(split(inverse), parts_a)
+    lower = wide([inverse, -weighted])
+    upper = wide([jnp.zeros_like(gram_a), eye(rank)]) - dot_split(parts_b, split(lower))
+    return split(jnp.concatenate([upper, lower], axis=0)), power
+
+
+def fused_kernel(depth, bases_ref, targets_ref, out_ref, flag_ref, *refs):
     levels, _, rank = bases_ref.shape
     half = rank // 2
     sums, taken = refs[:depth], refs[depth : 2 * depth]
-    coef, turned_ref, flag_own, flag_in = refs[2 * depth : 2 * depth + 4]
-    sems = refs[2 * depth + 4 :]
+    coef, turned_ref, moved, flag_own, flag_in = refs[2 * depth : 2 * depth + 5]
+    sems = refs[2 * depth + 5 :]
     link_send, link_recv, core_send, core_recv, relay_send, relay_recv, flag_send, flag_recv = sems
     me = lax.axis_index(AXIS)
     core = lax.rem(me, 2)
@@ -226,17 +236,42 @@
 
     links, swaps = {}, {}
 
+    def piece(row, number):
+        if number == 0:
+            return pl.ds(offset(row) + row + 1, 1)
+        return pl.ds(offset(row), row + 1)
+
+    def send_critical(bit, row):
+        for number in range(2):
+            region = (piece(row, number), own_half) if bit else (piece(row, number),)
+            src, dst = sums[bit].at[region], taken[bit].at[region]
+            send, recv = link_send.at[bit, number, row], link_recv.at[bit, number, row]
+            links[bit, row, number] = push(src, dst, send, recv, bit)
+            if bit:
+                send, recv = core_send.at[bit, number], core_recv.at[bit, number]
+                swaps[bit, number] = push(src, src, send, recv, 0)
+
     def send_row(bit, row):
-        slots = pl.ds(offset(row), row + 2)
-        critical = row == depth - 1 - bit
+        if row == depth - 1 - bit:
+            send_critical(bit, row)
+            return
+        region = (pl.ds(offset(row), row + 2), own_half if bit else other_half)
+        src, dst = sums[bit].at[region], taken[bit].at[region]
+        send, recv = link_send.at[bit, 0, row], link_recv.at[bit, 0, row]
+        links[bit, row] = push(src, dst, send, recv, bit)
+
+    def relay_piece(bit, row, number):
+        links[bit, row, number].wait_recv()
         if bit == 0:
-            region = (slots,) if critical else (slots, other_half)
-        else:
-            region = (slots, own_half)
-        src, dst = sums[bit].at[region], taken[bit].at[region]
-        links[bit, row] = push(src, dst, link_send.at[bit, row], link_recv.at[bit, row], bit)
-        if critical and bit:
-            swaps[bit] = push(src, src, core_send.at[bit], core_recv.at[bit], 0)
+            return None
+        region = taken[bit].at[piece(row, number), own_half]
+        send, recv = relay_send.at[bit, number], relay_recv.at[bit, number]
+        return push(region, region, send, recv, 0)
+
+    def finish_piece(bit, number, relay):
+        if relay is not None:
+            swaps[bit, number].wait_recv()
+            relay.wait_recv()
 
     parts = [split(targets_ref[...])] + [split(bases_ref[i]) for i in range(levels)]
     high, low = wide([part[0] for part in parts]), wide([part[1] for part in parts])
@@ -274,10 +309,8 @@
                 value = value - change[:, col * rank : (col + 1) * rank]
             sums[bit + 1][slot, own_half, :] = value
 
-    def changes(coef_a, coef_b, left_row, right_row):
-        proj_a, proj_b = left_row[:, :-rank], right_row[:, :-rank]
-        stacked = jnp.concatenate([coef_a, coef_b], axis=0)
-        rhs = split(jnp.concatenate([proj_a + coef_b, proj_b + coef_a], axis=0))
+    def changes(stacked, upper, lower):
+        rhs = split(jnp.concatenate([upper, lower], axis=0))
 
         def change_of(row):
             turned_ref[...] = stacked[:, (row + 1) * rank : (row + 2) * rank].T
@@ -301,40 +334,37 @@
             move_rows()
         change_of = lambda row: None
         if solving:
-            slots = pl.ds(offset(level_no), level_no + 2)
-            links[bit, level_no].wait_recv()
-            if bit:
-                region = taken[bit].at[slots, own_half]
-                relay = push(region, region, relay_send.at[bit], relay_recv.at[bit], 0)
+            base = offset(level_no)
+            is_left = side(bit) == 0
+
+            def both_sides(slots):
+                own = wide([sums[bit][slot] for slot in slots])
+                sib = wide([taken[bit][slot] for slot in slots])
+                return jnp.where(is_left, own, sib), jnp.where(is_left, sib, own)
+
+            relay = relay_piece(bit, level_no, 0)
+            finish_piece(bit, 0, relay)
+            gram_a, gram_b = both_sides([base + level_no + 1])
+            pair_inverse, power = inverse_of_pair(gram_a, gram_b)
+            relay = relay_piece(bit, level_no, 1)
             for row in late:
                 merge_row(bit - 1, row, late_change)
                 if row == rest[0]:
                     send_row(bit, row)
-            if bit:
-                swaps[bit].wait_recv()
-                relay.wait_recv()
-            base = offset(level_no)
-            own_row = wide([sums[bit][base + col] for col in range(level_no + 2)])
-            sib_row = wide([taken[bit][base + col] for col in range(level_no + 2)])
-            is_left = side(bit) == 0
-            left_row = jnp.where(is_left, own_row, sib_row)
-            right_row = jnp.where(is_left, sib_row, own_row)
-            state = []
-
-            def inverse_of(matrix):
-                inverse, power = fixed_inverse(matrix)
-                state.append(jnp.max((power * power).reshape(rank // 8, 8, rank), axis=0))
-                return inverse
-
-            coef_a, coef_b = solve_pair(left_row, right_row, inverse_of)
+            finish_piece(bit, 1, relay)
+            proj_a, proj_b = both_sides(range(base, base + level_no + 1))
+            stacked_proj = jnp.concatenate([proj_a, proj_b], axis=0)
+            stacked = dot_split(pair_inverse, split(stacked_proj))
+            coef_a, coef_b = stacked[:rank], stacked[rank:]
+            state = [jnp.max((power * power).reshape(rank // 8, 8, rank), axis=0)]
             flag = jnp.maximum(flag, state[0])
             own_coef = jnp.where(is_left, coef_a, coef_b)
             for col in range(level_no + 1):
                 coef[coef_slot(level_no, col)] = own_coef[:, col * rank : (col + 1) * rank]
             if level_no == 0:
-                last_ref[...] = own_coef
+                out_ref[...] = moved[:, :rank] - dot3(moved[:, rank:], own_coef)
             else:
-                change_of = changes(coef_a, coef_b, left_row, right_row)
+                change_of = changes(stacked, proj_a + coef_b, proj_b + coef_a)
         if rest:
             following = level_no - 1 < levels
             for row in rest[:1] if following else rest:
@@ -353,11 +383,6 @@
         copy.wait_send()
 
 
-def finish_kernel(moved_ref, last_ref, out_ref):
-    rank = last_ref.shape[0]
-    out_ref[...] = moved_ref[:, :rank] - dot3(moved_ref[:, rank:], last_ref[...])
-
-
 def fused(bases, targets, depth):
     levels, rows, rank = bases.shape
     stages = [
@@ -368,22 +393,23 @@
     return pl.pallas_call(
         functools.partial(fused_kernel, depth),
         out_shape=(
-            jax.ShapeDtypeStruct((rows, 2 * rank), jnp.float32),
-            jax.ShapeDtypeStruct((rank, rank), jnp.float32),
+            jax.ShapeDtypeStruct(targets.shape, jnp.float32),
             jax.ShapeDtypeStruct((8, 128), jnp.float32),
         ),
         in_specs=[VMEM_SPEC] * 2,
-        out_specs=(VMEM_SPEC,) * 3,
+        out_specs=(VMEM_SPEC,) * 2,
         scratch_shapes=stages
         + stages
         + [
             pltpu.VMEM((levels * (levels + 1) // 2, rank, rank), jnp.float32),
             pltpu.VMEM((rank, 2 * rank), jnp.float32),
+            pltpu.VMEM((rows, 2 * rank), jnp.float32),
             pltpu.VMEM((depth, 8, 128), jnp.float32),
             pltpu.VMEM((depth, 8, 128), jnp.float32),
         ]
-        + [dma((depth, levels))] * 2
-        + [dma((depth,))] * 6,
+        + [dma((depth, 2, levels))] * 2
+        + [dma((depth, 2))] * 4
+        + [dma((depth,))] * 2,
         compiler_params=pltpu.CompilerParams(
             collective_id=0, has_side_effects=True, vmem_limit_bytes=VMEM_LIMIT
         ),
@@ -412,13 +438,10 @@
 
 def per_device(bases, targets):
     depth = lax.axis_size(AXIS).bit_length() - 1
-    moved, last, residual = fused(bases, targets, depth)
+    out, residual = fused(bases, targets, depth)
     limit = (RESIDUAL / bases.shape[2]) ** 2
-    out = jax.ShapeDtypeStruct(targets.shape, jnp.float32)
     return lax.cond(
-        jnp.max(residual) < limit,
-        lambda: call(finish_kernel, out, (moved, last)),
-        lambda: general(bases, targets),
+        jnp.max(residual) < limit, lambda b, t, o: o, lambda b, t, o: general(b, t), bases, targets, out
     )
 
 

time: 51.7 us -> 56.9 us (1.10)
  Pallas kernels: 48.9 us -> 53.4 us
  local copies, waits for them, and re-layouts: 0.8 us -> 1.88 us
    pallas_call x1, Pallas kernels: 47.4 us -> 53.4 us  [fused(): pl.pallas_call(functools.partial(fused_kernel, depth), out_shape=(jax.Sha...]
    pallas_call x1 -> x0, Pallas kernels: 1.58 us -> none  [call(): pl.pallas_call(kernel, out_shape=outs, in_specs=[VMEM_SPEC] * len(args),...]
    unnamed x6 -> x5, local copies, waits for them, and re-layouts: 0.8 us -> 1.88 us
where the time goes in v3:
time: 56.9 us; the launch traced here: 56.8 us
  Pallas kernels  53.4 us (94%)
  local copies, waits for them, and re-layouts  1.88 us (3%)
  between operations  0.69 us (1%)
  other arithmetic  0.6 us (1%)
    pallas_call x1, Pallas kernels, fused(): pl.pallas_call(functools.partial(fused_kernel, depth), out_shape=(jax.Sha...  53.4 us
    unnamed x5, local copies, waits for them, and re-layouts  1.88 us

profile of v3, /device:TPU:0, one launch (start us, length us, event | category | flops | bytes accessed | tf_op | source)
XLA Modules:
  0.0 56.8 jit_solution(6280143289898653800)
XLA Ops:
  0.0 0.0 copy-start
  0.0 0.0 copy-start.1
  0.0 53.4 %shard_map.30 = (f32[1024,128]{1,0:T(8,128)}, f32[8,128]{1,0:T(8,128)S(1)}) custom-call(f32[5,1024,128]{2,1,0:T(8,128)} %bases_ref.1, f32[1024,128]{1,0:T(8,128)} %targets_ref.1), custom_call_target="tpu_custom_call" | custom-call | tf_op jit(solution)/shard_map/pallas_call | solution.py:393
  53.4 0.6 %reduce_max.9 = f32[]{:T(128)} reduce(f32[8,128]{1,0:T(8,128)S(1)} %get-tuple-element.25, f32[]{:T(128)} %constant.0.clone.1), dimensions={0,1}, to_apply=%region_0.0 | reduce | flops 1023 | bytes 4104 | tf_op jit(solution)/shard_map/reduce_max | solution.py:444
  54.6 0.0 copy-done
  54.6 0.0 copy-done.1
  54.7 0.2 conditional.1
  54.9 1.9 %copy.8 = f32[1024,128]{1,0:T(8,128)} copy(f32[1024,128]{1,0:T(8,128)} %get-tuple-element.27) | data formatting | bytes 1048576
Async XLA Ops:
  0.0 54.6 %copy-start = (f32[5,1024,128]{2,1,0:T(8,128)S(1)}, f32[5,1024,128]{2,1,0:T(8,128)}, u32[]{:S(2)}) copy-start(f32[5,1024,128]{2,1,0:T(8,128)} %bases_ref.1) | copy-start | bytes 7864324
  0.0 54.6 %copy-start.1 = (f32[1024,128]{1,0:T(8,128)S(1)}, f32[1024,128]{1,0:T(8,128)}, u32[]{:S(2)}) copy-start(f32[1024,128]{1,0:T(8,128)} %targets_ref.1) | copy-start | bytes 1572868

commit v4 on v2

--- a/solution.py
+++ b/solution.py
@@ -175,8 +175,8 @@
     return jax.ShapeDtypeStruct((count, rank, rank), jnp.float32)
 
 
-SQUARINGS = 4
-RESIDUAL = 1e-9
+SQUARINGS = 3
+RESIDUAL = 1e-7
 
 
 def fixed_inverse(matrix):
@@ -186,12 +186,12 @@
     return inverse, power
 
 
-def fused_kernel(depth, bases_ref, targets_ref, moved, last_ref, flag_ref, *refs):
+def fused_kernel(depth, bases_ref, targets_ref, out_ref, flag_ref, *refs):
     levels, _, rank = bases_ref.shape
     half = rank // 2
     sums, taken = refs[:depth], refs[depth : 2 * depth]
-    coef, turned_ref, flag_own, flag_in = refs[2 * depth : 2 * depth + 4]
-    sems = refs[2 * depth + 4 :]
+    coef, turned_ref, moved, flag_own, flag_in = refs[2 * depth : 2 * depth + 5]
+    sems = refs[2 * depth + 5 :]
     link_send, link_recv, core_send, core_recv, relay_send, relay_recv, flag_send, flag_recv = sems
     me = lax.axis_index(AXIS)
     core = lax.rem(me, 2)
@@ -237,6 +237,16 @@
         links[bit, row] = push(src, dst, link_send.at[bit, row], link_recv.at[bit, row], bit)
         if critical and bit:
             swaps[bit] = push(src, src, core_send.at[bit], core_recv.at[bit], 0)
+
+    def begin(bit, row):
+        if (bit, row) not in links:
+            send_row(bit, row)
+
+    def settle(bit, row):
+        copy = links[bit, row]
+        if bit and any(copy is other for other in pending):
+            copy.wait_send()
+            pending[:] = [other for other in pending if other is not copy]
 
     parts = [split(targets_ref[...])] + [split(bases_ref[i]) for i in range(levels)]
     high, low = wide([part[0] for part in parts]), wide([part[1] for part in parts])
@@ -301,15 +311,19 @@
             move_rows()
         change_of = lambda row: None
         if solving:
+            for place, row in enumerate(late):
+                settle(bit - 1, row)
+                if place + 1 < len(late):
+                    begin(bit - 1, late[place + 1])
+                merge_row(bit - 1, row, late_change)
+                if row == rest[0]:
+                    settle(bit, level_no)
+                    begin(bit, row)
             slots = pl.ds(offset(level_no), level_no + 2)
             links[bit, level_no].wait_recv()
             if bit:
                 region = taken[bit].at[slots, own_half]
                 relay = push(region, region, relay_send.at[bit], relay_recv.at[bit], 0)
-            for row in late:
-                merge_row(bit - 1, row, late_change)
-                if row == rest[0]:
-                    send_row(bit, row)
             if bit:
                 swaps[bit].wait_recv()
                 relay.wait_recv()
@@ -332,30 +346,25 @@
             for col in range(level_no + 1):
                 coef[coef_slot(level_no, col)] = own_coef[:, col * rank : (col + 1) * rank]
             if level_no == 0:
-                last_ref[...] = own_coef
+                out_ref[...] = moved[:, :rank] - dot3(moved[:, rank:], own_coef)
             else:
                 change_of = changes(coef_a, coef_b, left_row, right_row)
         if rest:
             following = level_no - 1 < levels
+            late = rest[1:] if following else []
+            late_change = change_of
+            if late:
+                settle(bit, rest[0])
+                begin(bit, late[0])
             for row in rest[:1] if following else rest:
                 merge_row(bit, row, change_of)
-                send_row(bit + 1, row)
-            late = rest[1:] if following else []
-            late_change = change_of
-            for row in late:
-                if (bit, row) not in links:
-                    send_row(bit, row)
+                begin(bit + 1, row)
         if bit:
             flag_copy.wait_recv()
             flag = jnp.maximum(flag, flag_in[bit])
     flag_ref[...] = flag
     for copy in pending:
         copy.wait_send()
-
-
-def finish_kernel(moved_ref, last_ref, out_ref):
-    rank = last_ref.shape[0]
-    out_ref[...] = moved_ref[:, :rank] - dot3(moved_ref[:, rank:], last_ref[...])
 
 
 def fused(bases, targets, depth):
@@ -368,17 +377,17 @@
     return pl.pallas_call(
         functools.partial(fused_kernel, depth),
         out_shape=(
-            jax.ShapeDtypeStruct((rows, 2 * rank), jnp.float32),
-            jax.ShapeDtypeStruct((rank, rank), jnp.float32),
+            jax.ShapeDtypeStruct(targets.shape, jnp.float32),
             jax.ShapeDtypeStruct((8, 128), jnp.float32),
         ),
         in_specs=[VMEM_SPEC] * 2,
-        out_specs=(VMEM_SPEC,) * 3,
+        out_specs=(VMEM_SPEC,) * 2,
         scratch_shapes=stages
         + stages
         + [
             pltpu.VMEM((levels * (levels + 1) // 2, rank, rank), jnp.float32),
             pltpu.VMEM((rank, 2 * rank), jnp.float32),
+            pltpu.VMEM((rows, 2 * rank), jnp.float32),
             pltpu.VMEM((depth, 8, 128), jnp.float32),
             pltpu.VMEM((depth, 8, 128), jnp.float32),
         ]
@@ -412,13 +421,10 @@
 
 def per_device(bases, targets):
     depth = lax.axis_size(AXIS).bit_length() - 1
-    moved, last, residual = fused(bases, targets, depth)
+    out, residual = fused(bases, targets, depth)
     limit = (RESIDUAL / bases.shape[2]) ** 2
-    out = jax.ShapeDtypeStruct(targets.shape, jnp.float32)
     return lax.cond(
-        jnp.max(residual) < limit,
-        lambda: call(finish_kernel, out, (moved, last)),
-        lambda: general(bases, targets),
+        jnp.max(residual) < limit, lambda b, t, o: o, lambda b, t, o: general(b, t), bases, targets, out
     )
 
 

time: 51.7 us -> 50.4 us (0.975)
  Pallas kernels: 48.9 us -> 46.5 us
  local copies, waits for them, and re-layouts: 0.8 us -> 1.88 us
    pallas_call x1 -> x0, Pallas kernels: 1.58 us -> none  [call(): pl.pallas_call(kernel, out_shape=outs, in_specs=[VMEM_SPEC] * len(args),...]
    unnamed x6 -> x5, local copies, waits for them, and re-layouts: 0.8 us -> 1.88 us
    pallas_call x1, Pallas kernels: 47.4 us -> 46.5 us  [fused(): pl.pallas_call(functools.partial(fused_kernel, depth), out_shape=(jax.Sha...]
where the time goes in v4:
time: 50.4 us; the launch traced here: 49.9 us
  Pallas kernels  46.5 us (92%)
  local copies, waits for them, and re-layouts  1.88 us (4%)
  between operations  0.69 us (1%)
  other arithmetic  0.6 us (1%)
    pallas_call x1, Pallas kernels, fused(): pl.pallas_call(functools.partial(fused_kernel, depth), out_shape=(jax.Sha...  46.5 us
    unnamed x5, local copies, waits for them, and re-layouts  1.88 us

profile of v4, /device:TPU:0, one launch (start us, length us, event | category | flops | bytes accessed | tf_op | source)
XLA Modules:
  0.0 49.9 jit_solution(2770836512580046638)
XLA Ops:
  0.0 0.0 copy-start
  0.0 0.0 copy-start.1
  0.0 46.5 %shard_map.30 = (f32[1024,128]{1,0:T(8,128)}, f32[8,128]{1,0:T(8,128)S(1)}) custom-call(f32[5,1024,128]{2,1,0:T(8,128)} %bases_ref.1, f32[1024,128]{1,0:T(8,128)} %targets_ref.1), custom_call_target="tpu_custom_call" | custom-call | tf_op jit(solution)/shard_map/pallas_call | solution.py:377
  46.5 0.6 %reduce_max.9 = f32[]{:T(128)} reduce(f32[8,128]{1,0:T(8,128)S(1)} %get-tuple-element.25, f32[]{:T(128)} %constant.0.clone.1), dimensions={0,1}, to_apply=%region_0.0 | reduce | flops 1023 | bytes 4104 | tf_op jit(solution)/shard_map/reduce_max | solution.py:427
  47.7 0.0 copy-done
  47.7 0.0 copy-done.1
  47.7 0.2 conditional.1
  48.0 1.9 %copy.8 = f32[1024,128]{1,0:T(8,128)} copy(f32[1024,128]{1,0:T(8,128)} %get-tuple-element.27) | data formatting | bytes 1048576
Async XLA Ops:
  0.0 47.7 %copy-start = (f32[5,1024,128]{2,1,0:T(8,128)S(1)}, f32[5,1024,128]{2,1,0:T(8,128)}, u32[]{:S(2)}) copy-start(f32[5,1024,128]{2,1,0:T(8,128)} %bases_ref.1) | copy-start | bytes 7864324
  0.0 47.7 %copy-start.1 = (f32[1024,128]{1,0:T(8,128)S(1)}, f32[1024,128]{1,0:T(8,128)}, u32[]{:S(2)}) copy-start(f32[1024,128]{1,0:T(8,128)} %targets_ref.1) | copy-start | bytes 1572868

commit v5 on v4

--- a/solution.py
+++ b/solution.py
@@ -9,6 +9,7 @@
 
 AXIS = "rows"
 VMEM_LIMIT = 48 * 2**20
+FUSED_LIMIT = 62 * 2**20
 VMEM_SPEC = pl.BlockSpec(memory_space=pltpu.VMEM)
 
 
@@ -186,12 +187,22 @@
     return inverse, power
 
 
-def fused_kernel(depth, bases_ref, targets_ref, out_ref, flag_ref, *refs):
-    levels, _, rank = bases_ref.shape
+def fused_kernel(depth, bases_in, targets_in, out_ref, flag_ref, *refs):
+    levels, _, rank = bases_in.shape
     half = rank // 2
     sums, taken = refs[:depth], refs[depth : 2 * depth]
     coef, turned_ref, moved, flag_own, flag_in = refs[2 * depth : 2 * depth + 5]
-    sems = refs[2 * depth + 5 :]
+    bases_ref, targets_ref, load = refs[2 * depth + 5 : 2 * depth + 8]
+    sems = refs[2 * depth + 8 :]
+    loads = [pltpu.make_async_copy(targets_in, targets_ref, load.at[levels])]
+    for level_no in range(levels):
+        loads.append(
+            pltpu.make_async_copy(
+                bases_in.at[level_no], bases_ref.at[level_no], load.at[level_no]
+            )
+        )
+    for copy in loads:
+        copy.start()
     link_send, link_recv, core_send, core_recv, relay_send, relay_recv, flag_send, flag_recv = sems
     me = lax.axis_index(AXIS)
     core = lax.rem(me, 2)
@@ -242,13 +253,10 @@
         if (bit, row) not in links:
             send_row(bit, row)
 
-    def settle(bit, row):
-        copy = links[bit, row]
-        if bit and any(copy is other for other in pending):
-            copy.wait_send()
-            pending[:] = [other for other in pending if other is not copy]
-
-    parts = [split(targets_ref[...])] + [split(bases_ref[i]) for i in range(levels)]
+    parts = []
+    for place, copy in enumerate(loads):
+        copy.wait()
+        parts.append(split(bases_ref[place - 1] if place else targets_ref[...]))
     high, low = wide([part[0] for part in parts]), wide([part[1] for part in parts])
     for row in reversed(range(levels)):
         end = (row + 2) * rank
@@ -311,19 +319,15 @@
             move_rows()
         change_of = lambda row: None
         if solving:
-            for place, row in enumerate(late):
-                settle(bit - 1, row)
-                if place + 1 < len(late):
-                    begin(bit - 1, late[place + 1])
+            for row in late:
                 merge_row(bit - 1, row, late_change)
-                if row == rest[0]:
-                    settle(bit, level_no)
-                    begin(bit, row)
             slots = pl.ds(offset(level_no), level_no + 2)
             links[bit, level_no].wait_recv()
             if bit:
                 region = taken[bit].at[slots, own_half]
                 relay = push(region, region, relay_send.at[bit], relay_recv.at[bit], 0)
+            for row in rest:
+                begin(bit, row)
             if bit:
                 swaps[bit].wait_recv()
                 relay.wait_recv()
@@ -353,9 +357,6 @@
             following = level_no - 1 < levels
             late = rest[1:] if following else []
             late_change = change_of
-            if late:
-                settle(bit, rest[0])
-                begin(bit, late[0])
             for row in rest[:1] if following else rest:
                 merge_row(bit, row, change_of)
                 begin(bit + 1, row)
@@ -380,7 +381,7 @@
             jax.ShapeDtypeStruct(targets.shape, jnp.float32),
             jax.ShapeDtypeStruct((8, 128), jnp.float32),
         ),
-        in_specs=[VMEM_SPEC] * 2,
+        in_specs=[pl.BlockSpec(memory_space=pl.ANY)] * 2,
         out_specs=(VMEM_SPEC,) * 2,
         scratch_shapes=stages
         + stages
@@ -390,11 +391,14 @@
             pltpu.VMEM((rows, 2 * rank), jnp.float32),
             pltpu.VMEM((depth, 8, 128), jnp.float32),
             pltpu.VMEM((depth, 8, 128), jnp.float32),
+            pltpu.VMEM(bases.shape, jnp.float32),
+            pltpu.VMEM(targets.shape, jnp.float32),
+            dma((levels + 1,)),
         ]
         + [dma((depth, levels))] * 2
         + [dma((depth,))] * 6,
         compiler_params=pltpu.CompilerParams(
-            collective_id=0, has_side_effects=True, vmem_limit_bytes=VMEM_LIMIT
+            collective_id=0, has_side_effects=True, vmem_limit_bytes=FUSED_LIMIT
         ),
     )(bases, targets)
 

time: 50.4 us -> 51.5 us (1.022)
  local copies, waits for them, and re-layouts: 1.88 us -> 0.8 us
  Pallas kernels: 46.5 us -> 47.5 us
  other arithmetic: 0.6 us -> 1.28 us
    unnamed x5 -> x3, local copies, waits for them, and re-layouts: 1.88 us -> 0.8 us
    pallas_call x1, Pallas kernels: 46.5 us -> 47.5 us  [fused(): pl.pallas_call(functools.partial(fused_kernel, depth), out_shape=(jax.Sha...]
    reduce_max x1, other arithmetic: 0.6 us -> 1.28 us  [per_device(): jnp.max(residual) < limit]
where the time goes in v5:
time: 51.5 us; the launch traced here: 50.5 us
  Pallas kernels  47.5 us (92%)
  other arithmetic  1.28 us (2%)
  local copies, waits for them, and re-layouts  0.8 us (2%)
  between operations  0.68 us (1%)
    pallas_call x1, Pallas kernels, fused(): pl.pallas_call(functools.partial(fused_kernel, depth), out_shape=(jax.Sha...  47.5 us
    reduce_max x1, other arithmetic, per_device(): jnp.max(residual) < limit  1.28 us

profile of v5, /device:TPU:0, one launch (start us, length us, event | category | flops | bytes accessed | tf_op | source)
XLA Modules:
  0.0 50.5 jit_solution(1071186946149385708)
XLA Ops:
  0.0 0.0 copy-start.1
  0.0 47.5 %shard_map.30 = (f32[1024,128]{1,0:T(8,128)S(1)}, f32[8,128]{1,0:T(8,128)}) custom-call(f32[5,1024,128]{2,1,0:T(8,128)} %bases_in.1, f32[1024,128]{1,0:T(8,128)} %targets_in.1), custom_call_target="tpu_custom_call" | custom-call | tf_op jit(solution)/shard_map/pallas_call | solution.py:378
  47.5 1.3 %reduce_max.9 = f32[]{:T(128)} reduce(f32[8,128]{1,0:T(8,128)} %get-tuple-element.25, f32[]{:T(128)} %constant.0.clone.1), dimensions={0,1}, to_apply=%region_0.0 | reduce | flops 1023 | bytes 4104 | tf_op jit(solution)/shard_map/reduce_max | solution.py:431
  49.5 0.0 copy-done.1
  49.5 0.2 conditional.1
  49.7 0.8 %copy.8 = f32[1024,128]{1,0:T(8,128)} copy(f32[1024,128]{1,0:T(8,128)S(1)} %get-tuple-element.27) | data formatting | bytes 1048576
Async XLA Ops:
  0.0 49.5 %copy-start.1 = (f32[1024,128]{1,0:T(8,128)S(1)}, f32[1024,128]{1,0:T(8,128)}, u32[]{:S(2)}) copy-start(f32[1024,128]{1,0:T(8,128)} %targets_in.1) | copy-start | bytes 1572868

commit v6 on v5

--- a/solution.py
+++ b/solution.py
@@ -253,6 +253,12 @@
         if (bit, row) not in links:
             send_row(bit, row)
 
+    def settle(bit, row):
+        copy = links[bit, row]
+        if bit and any(copy is other for other in pending):
+            copy.wait_send()
+            pending[:] = [other for other in pending if other is not copy]
+
     parts = []
     for place, copy in enumerate(loads):
         copy.wait()
@@ -319,15 +325,19 @@
             move_rows()
         change_of = lambda row: None
         if solving:
-            for row in late:
+            for place, row in enumerate(late):
+                settle(bit - 1, row)
+                if place + 1 < len(late):
+                    begin(bit - 1, late[place + 1])
                 merge_row(bit - 1, row, late_change)
+                if row == rest[0]:
+                    settle(bit, level_no)
+                    begin(bit, row)
             slots = pl.ds(offset(level_no), level_no + 2)
             links[bit, level_no].wait_recv()
             if bit:
                 region = taken[bit].at[slots, own_half]
                 relay = push(region, region, relay_send.at[bit], relay_recv.at[bit], 0)
-            for row in rest:
-                begin(bit, row)
             if bit:
                 swaps[bit].wait_recv()
                 relay.wait_recv()
@@ -357,13 +367,16 @@
             following = level_no - 1 < levels
             late = rest[1:] if following else []
             late_change = change_of
+            if late:
+                settle(bit, rest[0])
+                begin(bit, late[0])
             for row in rest[:1] if following else rest:
                 merge_row(bit, row, change_of)
                 begin(bit + 1, row)
         if bit:
             flag_copy.wait_recv()
             flag = jnp.maximum(flag, flag_in[bit])
-    flag_ref[...] = flag
+    flag_ref[0, 0] = jnp.sum(flag)
     for copy in pending:
         copy.wait_send()
 
@@ -379,10 +392,10 @@
         functools.partial(fused_kernel, depth),
         out_shape=(
             jax.ShapeDtypeStruct(targets.shape, jnp.float32),
-            jax.ShapeDtypeStruct((8, 128), jnp.float32),
+            jax.ShapeDtypeStruct((1, 1), jnp.float32),
         ),
         in_specs=[pl.BlockSpec(memory_space=pl.ANY)] * 2,
-        out_specs=(VMEM_SPEC,) * 2,
+        out_specs=(VMEM_SPEC, pl.BlockSpec(memory_space=pltpu.SMEM)),
         scratch_shapes=stages
         + stages
         + [
@@ -428,7 +441,7 @@
     out, residual = fused(bases, targets, depth)
     limit = (RESIDUAL / bases.shape[2]) ** 2
     return lax.cond(
-        jnp.max(residual) < limit, lambda b, t, o: o, lambda b, t, o: general(b, t), bases, targets, out
+        residual[0, 0] < limit, lambda b, t, o: o, lambda b, t, o: general(b, t), bases, targets, out
     )
 
 

time: 51.5 us -> 48.2 us (0.936); the launches traced: 50.5 us -> 48.1 us
  other arithmetic: 1.28 us -> 0 us
  Pallas kernels: 47.5 us -> 46.4 us
    reduce_max x1 -> x0, other arithmetic: 1.28 us -> none  [per_device(): jnp.max(residual) < limit]
    pallas_call x1, Pallas kernels: 47.5 us -> 46.4 us  [fused(): pl.pallas_call(functools.partial(fused_kernel, depth), out_shape=(jax.Sha...]
where the time goes in v6:
time: 48.2 us; the launch traced here: 48.1 us
  Pallas kernels  46.4 us (96%)
  local copies, waits for them, and re-layouts  0.8 us (2%)
  between operations  0.59 us (1%)
    pallas_call x1, Pallas kernels, fused(): pl.pallas_call(functools.partial(fused_kernel, depth), out_shape=(jax.Sha...  46.4 us

profile of v6, /device:TPU:0, one launch (start us, length us, event | category | flops | bytes accessed | tf_op | source)
XLA Modules:
  0.0 48.1 jit_solution(6630936877428865139)
XLA Ops:
  0.0 0.0 copy-start.1
  0.0 46.4 %shard_map.30 = (f32[1024,128]{1,0:T(8,128)S(1)}, f32[1,1]{1,0:T(1,128)}) custom-call(f32[5,1024,128]{2,1,0:T(8,128)} %bases_in.1, f32[1024,128]{1,0:T(8,128)} %targets_in.1), custom_call_target="tpu_custom_call" | custom-call | tf_op jit(solution)/shard_map/pallas_call | solution.py:391
  47.0 0.0 copy-done.1
  47.0 0.2 conditional.1
  47.3 0.8 %copy.8 = f32[1024,128]{1,0:T(8,128)} copy(f32[1024,128]{1,0:T(8,128)S(1)} %get-tuple-element.27) | data formatting | bytes 1048576
Async XLA Ops:
  0.0 47.0 %copy-start.1 = (f32[1024,128]{1,0:T(8,128)S(1)}, f32[1024,128]{1,0:T(8,128)}, u32[]{:S(2)}) copy-start(f32[1024,128]{1,0:T(8,128)} %targets_in.1) | copy-start | bytes 1572868

commit v7 on v6

--- a/solution.py
+++ b/solution.py
@@ -330,14 +330,13 @@
                 if place + 1 < len(late):
                     begin(bit - 1, late[place + 1])
                 merge_row(bit - 1, row, late_change)
-                if row == rest[0]:
-                    settle(bit, level_no)
-                    begin(bit, row)
             slots = pl.ds(offset(level_no), level_no + 2)
             links[bit, level_no].wait_recv()
             if bit:
                 region = taken[bit].at[slots, own_half]
                 relay = push(region, region, relay_send.at[bit], relay_recv.at[bit], 0)
+            if rest:
+                begin(bit, rest[0])
             if bit:
                 swaps[bit].wait_recv()
                 relay.wait_recv()

time: 48.2 us -> 48.6 us (level)
  no operation moved by 1% of the time
where the time goes in v7:
time: 48.6 us; the launch traced here: 48.4 us
  Pallas kernels  46.8 us (96%)
  local copies, waits for them, and re-layouts  0.8 us (2%)
  between operations  0.59 us (1%)
    pallas_call x1, Pallas kernels, fused(): pl.pallas_call(functools.partial(fused_kernel, depth), out_shape=(jax.Sha...  46.8 us

profile of v7, /device:TPU:0, one launch (start us, length us, event | category | flops | bytes accessed | tf_op | source)
XLA Modules:
  0.0 48.4 jit_solution(10264184849954305002)
XLA Ops:
  0.0 0.0 copy-start.1
  0.0 46.8 %shard_map.30 = (f32[1024,128]{1,0:T(8,128)S(1)}, f32[1,1]{1,0:T(1,128)}) custom-call(f32[5,1024,128]{2,1,0:T(8,128)} %bases_in.1, f32[1024,128]{1,0:T(8,128)} %targets_in.1), custom_call_target="tpu_custom_call" | custom-call | tf_op jit(solution)/shard_map/pallas_call | solution.py:390
  47.4 0.0 copy-done.1
  47.4 0.2 conditional.1
  47.6 0.8 %copy.8 = f32[1024,128]{1,0:T(8,128)} copy(f32[1024,128]{1,0:T(8,128)S(1)} %get-tuple-element.27) | data formatting | bytes 1048576
Async XLA Ops:
  0.0 47.4 %copy-start.1 = (f32[1024,128]{1,0:T(8,128)S(1)}, f32[1024,128]{1,0:T(8,128)}, u32[]{:S(2)}) copy-start(f32[1024,128]{1,0:T(8,128)} %targets_in.1) | copy-start | bytes 1572868
